TPU v7x, 32 devices: a whole 2x2x4 slice. The times are simulated.
32 devices in a mesh: dp: 2 (over x), mp: 16 (over z, y, core).
Axes of the slice: x: 2, y: 2, z: 4, core: 2. Of those that a mesh axis runs over, the one named last changes fastest.
Arguments:
- tokens: bfloat16 [512, 2048], P('dp'), may hold values from -6 to 6
- domain_ids: int32 [512], P('dp'), may hold values from 0 to 21
- domain_bias: bfloat16 [22, 2048], replicated, may hold values from -3 to 3
- dense_gate: bfloat16 [2048, 10944], P(None, 'mp'), may hold values from -0.125 to 0.125
- dense_up: bfloat16 [2048, 10944], P(None, 'mp'), may hold values from -0.125 to 0.125
- dense_down: bfloat16 [10944, 2048], P('mp'), may hold values from -0.0546875 to 0.0546875
- shared_gate: bfloat16 [2048, 2816], P(None, 'mp'), may hold values from -0.125 to 0.125
- shared_up: bfloat16 [2048, 2816], P(None, 'mp'), may hold values from -0.125 to 0.125
- shared_down: bfloat16 [2816, 2048], P('mp'), may hold values from -0.109375 to 0.109375
- expert_gate: bfloat16 [16, 2048, 1408], P('mp', None, 'dp'), may hold values from -0.125 to 0.125
- expert_up: bfloat16 [16, 2048, 1408], P('mp', None, 'dp'), may hold values from -0.125 to 0.125
- expert_down: bfloat16 [16, 1408, 2048], P('mp', 'dp'), may hold values from -0.15625 to 0.15625
- expert_ids: int32 [512, 6], P('dp'), may hold values from 0 to 15, all different within a row; in each aligned block of 16 rows (0 to 15, 16 to 31, ...) at most 12 rows name the same one
- route_weights: float32 [512, 6], P('dp'), may hold values from 0.05 to 0.6
Outputs:
- mixed: bfloat16 [512, 2048], P(('dp', 'mp'))
Inputs may be any that keep to these rules, and one draw needn't show every extreme that they name: `expert_ids`: each row names 6 different experts; in the 16 rows of one device (aligned blocks in order) no expert is named more than 12 times, and in some blocks one expert exactly 12 times.
All inputs are finite; a program needn't handle non-finite values.
Results may differ from a plain program's by a relative error of at most 0.009.
Values may be sent and summed in bfloat16 or wider, within the bound.
A program may use at most 128 MiB of HBM per device.

v0:
```python
import jax
import jax.numpy as jnp
from jax import lax
from jax.sharding import PartitionSpec as P


def swiglu(rows, w_gate, w_up):
    gate = jnp.dot(rows, w_gate, preferred_element_type=jnp.float32)
    up = jnp.dot(rows, w_up, preferred_element_type=jnp.float32)
    return (jax.nn.silu(gate) * up).astype(jnp.bfloat16)


def body(
    tokens,
    domain_ids,
    domain_bias,
    dense_gate,
    dense_up,
    dense_down,
    shared_gate,
    shared_up,
    shared_down,
    expert_gate,
    expert_up,
    expert_down,
    expert_ids,
    route_weights,
):
    width_mp = lax.axis_size("mp")
    column = lax.axis_index("mp")
    group_rows = tokens.shape[0]
    tok_dev = group_rows // width_mp
    topk = expert_ids.shape[1]
    most = min(tok_dev, max(2, -(-(2 * tok_dev * topk) // width_mp)))
    own_start = column * tok_dev
    lookup = (
        domain_ids[:, None] == jnp.arange(domain_bias.shape[0], dtype=jnp.int32)[None, :]
    ).astype(jnp.bfloat16)
    stream = (
        tokens.astype(jnp.float32)
        + jnp.dot(lookup, domain_bias, preferred_element_type=jnp.float32)
    ).astype(jnp.bfloat16)
    dense_hidden = swiglu(stream, dense_gate, dense_up)
    partial_sums = jnp.dot(dense_hidden, dense_down, preferred_element_type=jnp.float32)
    total = lax.psum(partial_sums, "mp")
    resid = (stream.astype(jnp.float32) + total).astype(jnp.bfloat16)
    own_resid = lax.dynamic_slice_in_dim(resid, own_start, tok_dev, 0)
    shared_hidden = swiglu(resid, shared_gate, shared_up)
    shared_part = jnp.dot(shared_hidden, shared_down, preferred_element_type=jnp.float32)
    hit = expert_ids == column
    chosen = jnp.any(hit, axis=1)
    blocks = chosen.reshape(width_mp, tok_dev).astype(jnp.int32)
    rank = jnp.cumsum(blocks, axis=1) - 1
    slots = jnp.arange(most, dtype=jnp.int32)
    pick = (blocks[:, None, :] == 1) & (rank[:, None, :] == slots[None, :, None])
    within = jnp.arange(tok_dev, dtype=jnp.int32)
    local = jnp.sum(jnp.where(pick, within[None, None, :], 0), axis=2)
    source = (local + jnp.arange(width_mp, dtype=jnp.int32)[:, None] * tok_dev).reshape(-1)
    filled = jnp.any(pick, axis=2).reshape(-1)
    picked = jnp.where(
        filled[:, None], jnp.take(resid, source, axis=0), jnp.zeros((), jnp.bfloat16)
    )
    w_gate = expert_gate[0]
    w_up = expert_up[0]
    w_down = expert_down[0]
    gathered_hidden = swiglu(lax.all_gather(picked, "dp", axis=0, tiled=True), w_gate, w_up)
    routed = lax.psum_scatter(
        jnp.dot(gathered_hidden, w_down, preferred_element_type=jnp.float32).astype(jnp.bfloat16),
        "dp",
        scatter_dimension=0,
        tiled=True,
    )
    shared_total = lax.psum_scatter(shared_part, "mp", scatter_dimension=0, tiled=True)
    arrived = lax.all_to_all(
        routed.reshape(width_mp, most, routed.shape[1]),
        "mp",
        split_axis=0,
        concat_axis=0,
        tiled=True,
    )
    own_ids = lax.dynamic_slice_in_dim(expert_ids, own_start, tok_dev, 0)
    own_weights = lax.dynamic_slice_in_dim(route_weights, own_start, tok_dev, 0)
    experts = jnp.arange(width_mp, dtype=jnp.int32)
    match = own_ids[:, :, None] == experts[None, None, :]
    named = jnp.any(match, axis=1).astype(jnp.int32)
    coef = jnp.sum(jnp.where(match, own_weights[:, :, None], 0.0), axis=1)
    own_rank = jnp.cumsum(named, axis=0) - 1
    placing = jnp.where(
        (named[:, :, None] == 1) & (own_rank[:, :, None] == slots[None, None, :]),
        coef[:, :, None],
        0.0,
    )
    routed_own = jnp.einsum(
        "tes,esd->td", placing, arrived.astype(jnp.float32), precision=lax.Precision.HIGHEST
    )
    mixed = own_resid.astype(jnp.float32) + shared_total + routed_own
    return mixed.astype(jnp.bfloat16)


def solution(mesh):
    return jax.shard_map(
        body,
        mesh=mesh,
        in_specs=(
            P("dp", None),
            P("dp"),
            P(),
            P(None, "mp"),
            P(None, "mp"),
            P("mp", None),
            P(None, "mp"),
            P(None, "mp"),
            P("mp", None),
            P("mp", None, "dp"),
            P("mp", None, "dp"),
            P("mp", "dp", None),
            P("dp", None),
            P("dp", None),
        ),
        out_specs=P(("dp", "mp"), None),
        check_vma=False,
    )
```

profile of v0, /device:TPU:0, one launch (start us, length us, event | category | flops | bytes accessed | tf_op | source)
XLA Modules:
  0.0 270.5 jit_solution(17580026948729388860)
XLA Ops:
  6.5 0.0 copy-start
  6.5 0.0 all-reduce.2.cloned.1.call-start
  6.5 1.9 fusion.9
  8.5 0.0 copy-start.1
  8.5 1.0 copy-done.1
  9.5 3.6 %fusion.53 = f32[256,684]{0,1:T(8,128)} fusion(bf16[256,2048]{1,0:T(8,128)(2,1)S(1)} %fusion.9, bf16[2048,684]{0,1:T(8,128)(2,1)} %param.17), kind=kOutput, calls=%fused_computation.70 | convolution fusion | flops 717225984 | bytes 4550656 | tf_op jit(solution)/shard_map/dot_general | solution.py:8
  13.1 7.8 %fusion.23 = f32[256,2048]{1,0:T(8,128)} fusion(bf16[684,2048]{1,0:T(8,128)(2,1)} %param.19, bf16[256,2048]{1,0:T(8,128)(2,1)} %copy-done.1, bf16[2048,684]{0,1:T(8,128)(2,1)} %param.18, f32[256,684]{0,1:T(8,128)} %fusion.53), kind=kOutput, calls=%fused_computation.21 | convolution fusion | flops 1435502592 | bytes 9449472 | tf_op jit(solution)/shard_map/dot_general | solution.py:44
  20.9 0.0 copy-start.2
  20.9 0.0 all-reduce.2.cloned.1.call-update
  20.9 0.0 all-gather.2.cloned.1.call-start
  20.9 0.6 copy-done.2
  21.6 0.1 reshape.88
  21.7 0.2 reduce_window_sum.23
  21.8 0.3 select_reduce_fusion
  22.1 0.1 copy.26
  22.2 0.1 add.101
  22.3 0.1 add.98
  22.4 0.3 fusion.41
  22.7 0.1 copy.25
  22.8 0.1 broadcast_in_dim.78
  23.0 98.6 %all-reduce.2.cloned.1.call-done = f32[256,2048]{1,0:T(8,128)} async-done(((f32[256,2048]{1,0:T(8,128)}), f32[256,2048]{1,0:T(8,128)}) %all-reduce.2.cloned.1.call-update) | async-done | bytes 2097168 | tf_op jit(solution)/shard_map/psum | solution.py:45
  121.5 3.1 %add_convert_fusion = bf16[256,2048]{1,0:T(8,128)(2,1)} fusion(f32[256,2048]{1,0:T(8,128)} %all-reduce.2.cloned.1.call-done, bf16[256,2048]{1,0:T(8,128)(2,1)} %copy-done.1), kind=kLoop, calls=%fused_computation.13 | loop fusion | flops 1572864 | bytes 4194304 | tf_op jit(solution)/shard_map/convert_element_type | solution.py:46
  124.7 4.2 %gather_fusion = bf16[192,2048]{1,0:T(8,128)(2,1)} fusion(bf16[256,2048]{1,0:T(8,128)(2,1)} %add_convert_fusion, s32[1024]{0:T(1024)S(1)} %pad_clamp_fusion), kind=kCustom, calls=%fused_computation | custom fusion | bytes 1573632 | tf_op jit(solution)/shard_map/jit(_take)/gather | solution.py:61
  128.8 2.2 select_select_fusion
  131.0 0.0 all-gather.2.cloned.1.call-update
  131.1 0.0 reduce-scatter.5.cloned.1.call-start
  131.1 26.6 %all-gather.2.cloned.1.call-done = bf16[384,2048]{1,0:T(8,128)(2,1)} async-done(((bf16[192,2048]{1,0:T(8,128)(2,1)}), bf16[384,2048]{1,0:T(8,128)(2,1)}) %all-gather.2.cloned.1.call-update) | async-done | bytes 1572880 | tf_op jit(solution)/shard_map/all_gather | solution.py:66
  157.7 5.0 %fusion.4 = f32[384,704]{0,1:T(8,128)} fusion(bf16[384,2048]{1,0:T(8,128)(2,1)} %all-gather.2.cloned.1.call-done, bf16[1,2048,704]{1,2,0:T(8,128)(2,1)} %param.23), kind=kOutput, calls=%fused_computation.5 | convolution fusion | flops 1107296256 | bytes 5537792 | tf_op jit(solution)/shard_map/dot_general | solution.py:8
  162.7 0.0 copy-done
  162.7 6.8 %fusion.6 = bf16[384,2048]{1,0:T(8,128)(2,1)} fusion(bf16[1,704,2048]{2,1,0:T(8,128)(2,1)S(1)} %copy-done, bf16[384,2048]{1,0:T(8,128)(2,1)} %all-gather.2.cloned.1.call-done, bf16[1,2048,704]{1,2,0:T(8,128)(2,1)} %param.24, f32[384,704]{0,1:T(8,128)} %fusion.4), kind=kOutput, calls=%fused_computation.7 | convolution fusion | flops 2217000960 | bytes 9994240 | tf_op jit(solution)/shard_map/dot_general | solution.py:68
  169.4 0.0 reduce-scatter.5.cloned.1.call-update
  169.5 0.0 reduce-scatter.3.cloned.1.call-start
  169.5 1.9 fusion.54
  171.4 4.4 %fusion.20 = f32[256,2048]{1,0:T(8,128)} fusion(bf16[176,2048]{1,0:T(8,128)(2,1)} %param.22, bf16[256,2048]{1,0:T(8,128)(2,1)} %add_convert_fusion, bf16[2048,176]{0,1:T(8,128)(2,1)} %param.21, f32[256,176]{0,1:T(8,128)S(1)} %fusion.54), kind=kOutput, calls=%fused_computation.20 | convolution fusion | flops 369369088 | bytes 4767744 | tf_op jit(solution)/shard_map/dot_general | solution.py:49
  175.8 0.0 reduce-scatter.3.cloned.1.call-update
  175.9 0.0 copy-start.3
  175.9 19.8 %reduce-scatter.5.cloned.1.call-done = bf16[192,2048]{1,0:T(8,128)(2,1)} async-done(((bf16[384,2048]{1,0:T(8,128)(2,1)}), bf16[192,2048]{1,0:T(8,128)(2,1)}) %reduce-scatter.5.cloned.1.call-update) | async-done | bytes 786448 | tf_op jit(solution)/shard_map/reduce_scatter | solution.py:67
  195.7 2.1 reshape.87
  197.8 5.7 %all-to-all-start = ((bf16[16,12,2048]{2,1,0:T(8,128)(2,1)}), bf16[16,12,2048]{2,1,0:T(8,128)(2,1)}, u32[]{:S(2)}, u32[]{:S(2)}) async-start(bf16[16,12,2048]{2,1,0:T(8,128)(2,1)} %reshape.87), calls=%async_computation.2 | async-start | bytes 2097152 | tf_op jit(solution)/shard_map/all_to_all | solution.py:74
  203.5 0.1 constant_dynamic-slice_fusion.1
  203.6 0.1 fusion.47
  203.7 0.0 copy-done.3
  203.7 0.1 constant_dynamic-slice_fusion
  203.8 0.1 select_reduce_fusion.1
  203.9 57.0 %reduce-scatter.3.cloned.1.call-done = f32[16,2048]{1,0:T(8,128)} async-done(((f32[256,2048]{1,0:T(8,128)}), f32[16,2048]{1,0:T(8,128)}) %reduce-scatter.3.cloned.1.call-update) | async-done | bytes 131088 | tf_op jit(solution)/shard_map/reduce_scatter | solution.py:73
  260.9 0.0 all-to-all-done
  260.9 3.0 %fusion.11 = bf16[16,2048]{1,0:T(8,128)(2,1)} fusion(bf16[16,12,2048]{2,1,0:T(8,128)(2,1)} %all-to-all-done, f32[16,2048]{1,0:T(8,128)} %reduce-scatter.3.cloned.1.call-done, bf16[256,2048]{1,0:T(8,128)(2,1)} %add_convert_fusion, s32[]{:T(128)S(6)} %select_n.41, f32[16,16]{1,0:T(8,128)S(1)} %select_reduce_fusion.1, s32[16,16]{1,0:T(8,128)S(1)} %broadcast_add_fusion.2, ...), kind=kOutput, calls=%fused_computation.12 | convolution fusion | flops 75637760 | bytes 1050884 | tf_op jit(solution)/shard_map/tes,esd->td/dot_general | solution.py:93
  (12 shorter events, 0.1 us)
Async XLA Ops:
  6.5 156.1 %copy-start = (bf16[1,704,2048]{2,1,0:T(8,128)(2,1)S(1)}, bf16[1,704,2048]{2,1,0:T(8,128)(2,1)}, u32[]{:S(2)}) copy-start(bf16[1,704,2048]{2,1,0:T(8,128)(2,1)} %param.25) | copy-start | bytes 8650756
  6.5 115.0 %all-reduce.2.cloned.1.call-start = ((), (), s32[]{:S(2)}) async-start(), calls=%async_computation.3 | async-start | bytes 4194304 | tf_op jit(solution)/shard_map/psum | solution.py:45
  8.5 1.0 copy-start.1
  20.9 0.7 copy-start.2
  20.9 136.8 %all-gather.2.cloned.1.call-start = ((), (), s32[]{:S(2)}) async-start(), calls=%async_computation.5 | async-start | bytes 2359296 | tf_op jit(solution)/shard_map/all_gather | solution.py:66
  131.1 64.6 %reduce-scatter.5.cloned.1.call-start = ((), (), s32[]{:S(2)}) async-start(), calls=%async_computation.6 | async-start | bytes 2359296 | tf_op jit(solution)/shard_map/reduce_scatter | solution.py:67
  169.5 91.4 %reduce-scatter.3.cloned.1.call-start = ((), (), s32[]{:S(2)}) async-start(), calls=%async_computation.4 | async-start | bytes 2228224 | tf_op jit(solution)/shard_map/reduce_scatter | solution.py:73
  175.9 27.9 %copy-start.3 = (f32[256,6]{0,1:T(8,128)S(1)}, f32[256,6]{0,1:T(8,128)}, u32[]{:S(2)}) copy-start(f32[256,6]{0,1:T(8,128)} %param.27) | copy-start | bytes 18436
  197.8 63.1 %all-to-all-start = ((bf16[16,12,2048]{2,1,0:T(8,128)(2,1)}), bf16[16,12,2048]{2,1,0:T(8,128)(2,1)}, u32[]{:S(2)}, u32[]{:S(2)}) async-start(bf16[16,12,2048]{2,1,0:T(8,128)(2,1)} %reshape.87), calls=%async_computation.2 | async-start | bytes 2097152 | tf_op jit(solution)/shard_map/all_to_all | solution.py:74
Sparse Core Ops, SparseCore 0:
  21.0 100.4 all-reduce.1
  131.2 26.4 all-gather.1
  169.6 26.0 reduce-scatter.4
  199.3 61.5 reduce-scatter.2
where the time goes:
time: 271 us; the launch traced here: 270 us
  waiting for transfers between devices  202 us (75%)
  matrix products  34.4 us (13%)
  between operations  13.2 us (5%)
  local copies, waits for them, and re-layouts  8.64 us (3%)
  other arithmetic  6.36 us (2%)
  starting transfers between devices  5.8 us (2%)
    psum x1, waiting for transfers between devices, body(): total = lax.psum(partial_sums, 'mp')  98.6 us
    reduce_scatter x1, waiting for transfers between devices, body(): lax.psum_scatter(shared_part, 'mp', scatter_dimension=0, tiled=True)  57 us
    all_gather x1, waiting for transfers between devices, body(): lax.all_gather(picked, 'dp', axis=0, tiled=True)  26.6 us
    reduce_scatter x1, waiting for transfers between devices, body(): lax.psum_scatter(jnp.dot(gathered_hidden, w_down, preferred_element_type=...  19.8 us
    dot_general x3, matrix products, swiglu(): gate = jnp.dot(rows, w_gate, preferred_element_type=jnp.float32)  10.5 us
    dot_general x1, matrix products, body(): jnp.dot(dense_hidden, dense_down, preferred_element_type=jnp.float32)  7.78 us
    dot_general x1, matrix products, body(): jnp.dot(gathered_hidden, w_down, preferred_element_type=jnp.float32)  6.75 us
    all_to_all x1, starting transfers between devices, body(): lax.all_to_all(routed.reshape(width_mp, most, routed.shape[1]), 'mp', spl...  5.67 us
  transfers between devices with their start and end apart: 5, of which 4 were waited for; matrix products, arithmetic and copies ran while one was open for 4% of the time, Pallas kernels for 0%

commit v1 on v0

v1 whole, which is shorter than its diff:
```python
import functools

import jax
import jax.numpy as jnp
from jax import lax
from jax.experimental import pallas as pl
from jax.experimental.pallas import tpu as pltpu
from jax.sharding import PartitionSpec as P

F32 = jnp.float32
BF16 = jnp.bfloat16
CORES = 2
CHUNKS = 4
ROW_TILE = 256
COL_TILE = 256


def dot(a, b):
    return jnp.dot(a, b, preferred_element_type=F32)


def kernel(
    n_dp,
    n_mp,
    tokens,
    domain_ids,
    domain_bias,
    dense_gate,
    dense_up,
    dense_down,
    shared_gate,
    shared_up,
    shared_down,
    expert_gate,
    expert_up,
    expert_down,
    expert_ids,
    route_weights,
    out,
    stream,
    wdg,
    wdu,
    wdd,
    wsg,
    wsu,
    wsd,
    weg,
    weu,
    wed,
    dense_hid,
    shared_hid,
    expert_hid,
    coef,
    part,
    resid,
    pair1,
    plane1,
    pair2,
    cross,
    plane2,
    load_sem,
    coef_ss,
    coef_rs,
    pair1_ss,
    pair1_rs,
    plane1_ss,
    plane1_rs,
    ring_ss,
    ring_rs,
    sib_ss,
    sib_rs,
    dup_ss,
    dup_rs,
    pair2_ss,
    pair2_rs,
    cross_ss,
    cross_rs,
    plane2_ss,
    plane2_rs,
):
    group = lax.axis_index("dp")
    column = lax.axis_index("mp")
    chip = column // CORES
    core = lax.rem(column, CORES)
    other = 1 - core
    chips = n_mp // CORES
    rows, width = stream.shape
    block = rows // n_mp
    tile = min(rows, ROW_TILE)
    tiles = rows // tile
    tile_chips = tile // (CORES * block)
    cols = width // CHUNKS
    sibling = (group, chip * CORES + other)

    def chip_at(j):
        return lax.rem(chip + j, chips)

    def chip_from(j):
        return lax.rem(chip + (chips - j), chips)

    def group_at(i):
        return lax.rem(group + i, n_dp)

    def group_from(i):
        return lax.rem(group + (n_dp - i), n_dp)

    def peer(j):
        return (group, chip_at(j) * CORES + core)

    def partner(i):
        return (group_at(i), column)

    def remote(src, dst, ss, rs, device):
        return pltpu.make_async_remote_copy(
            src_ref=src,
            dst_ref=dst,
            send_sem=ss,
            recv_sem=rs,
            device_id=device,
            device_id_type=pl.DeviceIdType.MESH,
        )

    def each_tile(fn):
        if tiles == 1:
            fn(0)
        else:
            pl.loop(0, tiles)(fn)

    def row_span(t):
        return pl.ds(t * tile, tile) if tiles == 1 else pl.ds(pl.multiple_of(t * tile, tile), tile)

    def chip_span(t):
        return pl.ds(t * tile_chips, tile_chips)

    loads = []
    for index, (src, dst) in enumerate(
        (
            (tokens, stream),
            (dense_gate, wdg),
            (dense_up, wdu),
            (dense_down, wdd),
            (shared_gate, wsg),
            (shared_up, wsu),
            (shared_down, wsd),
            (expert_gate.at[0], weg),
            (expert_up.at[0], weu),
            (expert_down.at[0], wed),
        )
    ):
        load = pltpu.make_async_copy(src, dst, load_sem.at[index])
        load.start()
        loads.append(load)

    barrier = pltpu.get_barrier_semaphore()
    contacts = [sibling]
    contacts += [peer(j) for j in range(1, chips)]
    contacts += [partner(i) for i in range(1, n_dp)]
    for device in contacts:
        pl.semaphore_signal(barrier, inc=1, device_id=device, device_id_type=pl.DeviceIdType.MESH)

    named = expert_ids[...] == column
    own_coef = jnp.sum(jnp.where(named, route_weights[...], 0.0), axis=1, keepdims=True)
    coef[group] = jnp.broadcast_to(own_coef, coef.shape[1:])

    loads[0].wait()

    domains = domain_bias.shape[0]

    def add_bias(t):
        span = row_span(t)
        numbers = lax.broadcasted_iota(jnp.int32, (tile, domains), 1)
        lookup = jnp.where(domain_ids[span, :] == numbers, 1.0, 0.0).astype(BF16)
        stream[span, :] = (
            stream[span, :].astype(F32) + dot(lookup, domain_bias[...])
        ).astype(BF16)

    each_tile(add_bias)

    def swiglu(read, w_gate, w_up, hidden):
        units = w_gate.shape[1]

        def one(t):
            span = row_span(t)
            x = read(t)
            for start in range(0, units, COL_TILE):
                stop = min(units, start + COL_TILE)
                gate = dot(x, w_gate[:, start:stop])
                up = dot(x, w_up[:, start:stop])
                hidden[span, start:stop] = (gate / (1.0 + jnp.exp(-gate)) * up).astype(BF16)

        each_tile(one)

    loads[1].wait()
    loads[2].wait()
    swiglu(lambda t: stream[row_span(t), :], wdg, wdu, dense_hid)

    pl.semaphore_wait(barrier, len(contacts))
    coef_sends = [
        remote(coef.at[group], coef.at[group], coef_ss.at[i - 1], coef_rs.at[i - 1], partner(i))
        for i in range(1, n_dp)
    ]
    for copy in coef_sends:
        copy.start()

    loads[3].wait()
    pair_sends = []
    for h in range(CHUNKS):
        span = slice(h * cols, (h + 1) * cols)

        def down(t):
            value = dot(dense_hid[row_span(t), :], wdd[:, span])
            part[chip_span(t), :, :, span] = value.astype(BF16).reshape(
                tile_chips, CORES, block, cols
            )

        each_tile(down)
        copy = remote(
            part.at[:, other, :, span],
            pair1.at[:, :, span],
            pair1_ss.at[h],
            pair1_rs.at[h],
            sibling,
        )
        copy.start()
        pair_sends.append(copy)
    for copy in pair_sends:
        copy.wait_recv()
    plane_sends = []
    for j in range(1, chips):
        k = chip_at(j)
        part[k, core] = (part[k, core].astype(F32) + pair1[k].astype(F32)).astype(BF16)
        copy = remote(
            part.at[k, core], plane1.at[j], plane1_ss.at[j], plane1_rs.at[j], peer(j)
        )
        copy.start()
        plane_sends.append(copy)
    own_rows = pl.ds(pl.multiple_of(column * block, block), block)
    total = part[chip, core].astype(F32) + pair1[chip].astype(F32)
    for j in range(1, chips):
        plane_sends[j - 1].wait_recv()
        total = total + plane1[j].astype(F32)
    resid[group, chip, core] = (stream[own_rows, :].astype(F32) + total).astype(BF16)

    ring_sends, sib_sends, dup_sends = [], [], []

    def spread(j):
        k = chip_from(j)
        mine = resid.at[group, k, core]
        for i in range(1, n_dp):
            copy = remote(mine, mine, dup_ss.at[i - 1, j], dup_rs.at[i - 1, j], partner(i))
            copy.start()
            dup_sends.append(copy)
        copy = remote(mine, mine, sib_ss.at[0, j], sib_rs.at[0, j], sibling)
        copy.start()
        sib_sends.append(copy)

    own = resid.at[group, chip, core]
    for j in range(1, chips):
        copy = remote(own, own, ring_ss.at[j], ring_rs.at[j], peer(j))
        copy.start()
        ring_sends.append(copy)
    spread(0)
    for j in range(1, chips):
        landed = resid.at[group, chip_from(j), core]
        remote(landed, landed, ring_ss.at[j], ring_rs.at[j], peer(j)).wait_recv()
        spread(j)

    def from_sibling(i):
        for j in range(chips):
            landed = resid.at[group_from(i), chip_from(j), other]
            remote(landed, landed, sib_ss.at[i, j], sib_rs.at[i, j], sibling).wait_recv()

    def group_rows(g):
        return lambda t: resid[g, chip_span(t)].reshape(tile, width)

    from_sibling(0)
    for index in (4, 5, 7, 8):
        loads[index].wait()
    swiglu(group_rows(group), wsg, wsu, shared_hid)
    for i in range(1, n_dp):
        for j in range(chips):
            landed = resid.at[group_from(i), chip_from(j), core]
            remote(
                landed, landed, dup_ss.at[i - 1, j], dup_rs.at[i - 1, j], partner(i)
            ).wait_recv()
            copy = remote(landed, landed, sib_ss.at[i, j], sib_rs.at[i, j], sibling)
            copy.start()
            sib_sends.append(copy)
    for copy in coef_sends:
        copy.wait()
    loads[6].wait()
    loads[9].wait()
    for copy in pair_sends + plane_sends + ring_sends + dup_sends:
        copy.wait_send()

    cross_sends, pair2_sends = [], []
    for i in range(1, n_dp):
        from_sibling(i)
    for copy in sib_sends:
        copy.wait_send()
    for i in range(1, n_dp):
        g = group_from(i)
        swiglu(group_rows(g), weg, weu, expert_hid)
        sends = []
        for h in range(CHUNKS):
            span = slice(h * cols, (h + 1) * cols)

            def down_other(t):
                value = coef[g, row_span(t), 0:1] * dot(expert_hid[row_span(t), :], wed[:, span])
                resid[g, chip_span(t), :, :, span] = value.astype(BF16).reshape(
                    tile_chips, CORES, block, cols
                )

            each_tile(down_other)
            copy = remote(
                resid.at[g, :, other, :, span],
                pair2.at[i, :, :, span],
                pair2_ss.at[i, h],
                pair2_rs.at[i, h],
                sibling,
            )
            copy.start()
            sends.append(copy)
        for copy in sends:
            copy.wait_recv()
        pair2_sends += sends
        for j in range(chips):
            k = chip_at(j)
            resid[g, k, core] = (
                resid[g, k, core].astype(F32) + pair2[i, k].astype(F32)
            ).astype(BF16)
            copy = remote(
                resid.at[g, k, core],
                cross.at[i - 1, k],
                cross_ss.at[i - 1, j],
                cross_rs.at[i - 1, j],
                (g, column),
            )
            copy.start()
            cross_sends.append(copy)

    swiglu(group_rows(group), weg, weu, expert_hid)
    sends = []
    for h in range(CHUNKS):
        span = slice(h * cols, (h + 1) * cols)

        def down_own(t):
            value = dot(shared_hid[row_span(t), :], wsd[:, span])
            value = value + coef[group, row_span(t), 0:1] * dot(
                expert_hid[row_span(t), :], wed[:, span]
            )
            part[chip_span(t), :, :, span] = value.astype(BF16).reshape(
                tile_chips, CORES, block, cols
            )

        each_tile(down_own)
        copy = remote(
            part.at[:, other, :, span],
            pair2.at[0, :, :, span],
            pair2_ss.at[0, h],
            pair2_rs.at[0, h],
            sibling,
        )
        copy.start()
        sends.append(copy)
    for copy in sends:
        copy.wait_recv()
    pair2_sends += sends
    plane_sends = []
    total = None
    for j in list(range(1, chips)) + [0]:
        k = chip_at(j)
        value = part[k, core].astype(F32) + pair2[0, k].astype(F32)
        for i in range(1, n_dp):
            landed = cross.at[i - 1, k]
            remote(
                landed, landed, cross_ss.at[i - 1, j], cross_rs.at[i - 1, j], partner(i)
            ).wait_recv()
            value = value + cross[i - 1, k].astype(F32)
        if j == 0:
            total = value
            continue
        part[k, core] = value.astype(BF16)
        copy = remote(
            part.at[k, core], plane2.at[j], plane2_ss.at[j], plane2_rs.at[j], peer(j)
        )
        copy.start()
        plane_sends.append(copy)
    total = total + resid[group, chip, core].astype(F32)
    for j in range(1, chips):
        plane_sends[j - 1].wait_recv()
        total = total + plane2[j].astype(F32)
    out[...] = total.astype(BF16)
    for copy in plane_sends + pair2_sends + cross_sends:
        copy.wait_send()


def body(n_dp, n_mp, *args):
    (
        tokens,
        domain_ids,
        domain_bias,
        dense_gate,
        dense_up,
        dense_down,
        shared_gate,
        shared_up,
        shared_down,
        expert_gate,
        expert_up,
        expert_down,
        expert_ids,
        route_weights,
    ) = args
    rows, width = tokens.shape
    block = rows // n_mp
    chips = n_mp // CORES
    ff, sh, eh = dense_gate.shape[1], shared_gate.shape[1], expert_gate.shape[2]
    others = max(1, n_dp - 1)
    dma = pltpu.SemaphoreType.DMA
    vmem = pl.BlockSpec(memory_space=pltpu.VMEM)
    hbm = pl.BlockSpec(memory_space=pl.ANY)
    flops = 6 * width * rows * (ff + sh + n_dp * eh)
    moved = 6 * width * (ff + sh + eh)
    return pl.pallas_call(
        functools.partial(kernel, n_dp, n_mp),
        out_shape=jax.ShapeDtypeStruct((block, width), BF16),
        in_specs=[hbm, vmem, vmem] + [hbm] * 9 + [vmem, vmem],
        out_specs=vmem,
        scratch_shapes=[
            pltpu.VMEM((rows, width), BF16),
            pltpu.VMEM((width, ff), BF16),
            pltpu.VMEM((width, ff), BF16),
            pltpu.VMEM((ff, width), BF16),
            pltpu.VMEM((width, sh), BF16),
            pltpu.VMEM((width, sh), BF16),
            pltpu.VMEM((sh, width), BF16),
            pltpu.VMEM((width, eh), BF16),
            pltpu.VMEM((width, eh), BF16),
            pltpu.VMEM((eh, width), BF16),
            pltpu.VMEM((rows, ff), BF16),
            pltpu.VMEM((rows, sh), BF16),
            pltpu.VMEM((rows, eh), BF16),
            pltpu.VMEM((n_dp, rows, 128), F32),
            pltpu.VMEM((chips, CORES, block, width), BF16),
            pltpu.VMEM((n_dp, chips, CORES, block, width), BF16),
            pltpu.VMEM((chips, block, width), BF16),
            pltpu.VMEM((chips, block, width), BF16),
            pltpu.VMEM((n_dp, chips, block, width), BF16),
            pltpu.VMEM((others, chips, block, width), BF16),
            pltpu.VMEM((chips, block, width), BF16),
            dma((10,)),
            dma((others,)),
            dma((others,)),
            dma((CHUNKS,)),
            dma((CHUNKS,)),
            dma((chips,)),
            dma((chips,)),
            dma((chips,)),
            dma((chips,)),
            dma((n_dp, chips)),
            dma((n_dp, chips)),
            dma((others, chips)),
            dma((others, chips)),
            dma((n_dp, CHUNKS)),
            dma((n_dp, CHUNKS)),
            dma((others, chips)),
            dma((others, chips)),
            dma((chips,)),
            dma((chips,)),
        ],
        compiler_params=pltpu.CompilerParams(
            collective_id=0,
            has_side_effects=True,
            vmem_limit_bytes=63 * 1024 * 1024,
        ),
        cost_estimate=pl.CostEstimate(flops=flops, bytes_accessed=moved, transcendentals=0),
    )(
        tokens,
        domain_ids.reshape(rows, 1),
        domain_bias,
        dense_gate,
        dense_up,
        dense_down,
        shared_gate,
        shared_up,
        shared_down,
        expert_gate,
        expert_up,
        expert_down,
        expert_ids,
        route_weights,
    )


def solution(mesh):
    n_dp, n_mp = mesh.shape["dp"], mesh.shape["mp"]
    return jax.shard_map(
        functools.partial(body, n_dp, n_mp),
        mesh=mesh,
        in_specs=(
            P("dp", None),
            P("dp"),
            P(),
            P(None, "mp"),
            P(None, "mp"),
            P("mp", None),
            P(None, "mp"),
            P(None, "mp"),
            P("mp", None),
            P("mp", None, "dp"),
            P("mp", None, "dp"),
            P("mp", "dp", None),
            P("dp", None),
            P("dp", None),
        ),
        out_specs=P(("dp", "mp"), None),
        check_vma=False,
    )
```

time: 271 us -> 96.4 us (0.36)
  waiting for transfers between devices: 202 us -> 0 us
  Pallas kernels: 0 us -> 69.3 us
  matrix products: 34.4 us -> 0 us
  local copies, waits for them, and re-layouts: 8.64 us -> 25.5 us
  between operations: 13.2 us -> 0.02 us
  other arithmetic: 6.36 us -> 0 us
  starting transfers between devices: 5.8 us -> 0 us
    psum x1 -> x0, waiting for transfers between devices: 98.6 us -> none  [body(): total = lax.psum(partial_sums, 'mp')]
    reduce_scatter x2 -> x0, waiting for transfers between devices: 76.8 us -> none  [the longest x1 57 us: body(): lax.psum_scatter(shared_part, 'mp', scatter_dimension=0, tiled=True)]
    pallas_call x0 -> x1, Pallas kernels: none -> 69.3 us  [body(): pl.pallas_call(functools.partial(kernel, n_dp, n_mp), out_shape=jax.Shape...]
    dot_general x8 -> x0, matrix products: 34.4 us -> none  [the longest x3 10.5 us: swiglu(): gate = jnp.dot(rows, w_gate, preferred_element_type=jnp.float32)]
    all_gather x1 -> x0, waiting for transfers between devices: 26.6 us -> none  [body(): lax.all_gather(picked, 'dp', axis=0, tiled=True)]
    unnamed x8 -> x13, local copies, waits for them, and re-layouts: 1.66 us -> 23.9 us
    all_to_all x1 -> x0, starting transfers between devices: 5.67 us -> none  [body(): lax.all_to_all(routed.reshape(width_mp, most, routed.shape[1]), 'mp', spl...]
    gather x1 -> x0, local copies, waits for them, and re-layouts: 4.16 us -> none  [body(): jnp.take(resid, source, axis=0)]
  transfers between devices with their start and end apart: 5 -> 0, of which waited for: 4 -> 0; matrix products, arithmetic and copies ran while one was open for 4% -> 0% of each run, Pallas kernels for 0% -> 0%
where the time goes in v1:
time: 96.4 us; the launch traced here: 94.8 us
  Pallas kernels  69.3 us (72%)
  local copies, waits for them, and re-layouts  25.5 us (26%)
    pallas_call x1, Pallas kernels, body(): pl.pallas_call(functools.partial(kernel, n_dp, n_mp), out_shape=jax.Shape...  69.3 us
    unnamed x13, local copies, waits for them, and re-layouts  23.9 us

profile of v1, /device:TPU:0, one launch (start us, length us, event | category | flops | bytes accessed | tf_op | source)
XLA Modules:
  0.0 94.8 jit_solution(7426358954130538615)
XLA Ops:
  0.0 0.0 copy-start.1
  0.0 1.6 %copy.23.domain_ids = s32[256,1]{1,0:T(8,128)} copy(s32[256,1]{0,1:T(1,128)} %bitcast.1) | data formatting | bytes 2048 | tf_op jit(solution)/shard_map/reshape | solution.py:480
  1.6 1.5 %copy.30.expert_ids = s32[256,6]{1,0:T(8,128)} copy(s32[256,6]{0,1:T(8,128)} %param.26) | data formatting | bytes 12288 | tf_op args[12]
  3.1 1.5 %copy.31.route_weights = f32[256,6]{1,0:T(8,128)} copy(f32[256,6]{0,1:T(8,128)} %param.27) | data formatting | bytes 12288 | tf_op args[13]
  4.6 2.2 %copy.26.shared_gate = bf16[2048,176]{1,0:T(8,128)(2,1)} copy(bf16[2048,176]{0,1:T(8,128)(2,1)} %param.20) | data formatting | bytes 1441792 | tf_op args[6]
  6.8 2.2 %copy.27.shared_up = bf16[2048,176]{1,0:T(8,128)(2,1)} copy(bf16[2048,176]{0,1:T(8,128)(2,1)} %param.21) | data formatting | bytes 1441792 | tf_op args[7]
  9.0 0.0 copy-done.1
  9.0 2.8 %copy.24.dense_gate = bf16[2048,684]{1,0:T(8,128)(2,1)} copy(bf16[2048,684]{0,1:T(8,128)(2,1)S(1)} %copy-done.1) | data formatting | bytes 5603328 | tf_op args[3]
  11.8 0.0 copy-start
  11.8 4.8 %copy.25.dense_up = bf16[2048,684]{1,0:T(8,128)(2,1)} copy(bf16[2048,684]{0,1:T(8,128)(2,1)} %param.18) | data formatting | bytes 5603328 | tf_op args[4]
  16.6 0.0 copy-done
  16.6 2.9 %copy.28.expert_gate = bf16[1,2048,704]{2,1,0:T(8,128)(2,1)} copy(bf16[1,2048,704]{1,2,0:T(8,128)(2,1)S(1)} %copy-done) | data formatting | bytes 5767168 | tf_op args[9]
  19.4 4.6 %copy.29.expert_up = bf16[1,2048,704]{2,1,0:T(8,128)(2,1)} copy(bf16[1,2048,704]{1,2,0:T(8,128)(2,1)} %param.24) | data formatting | bytes 5767168 | tf_op args[10]
  24.0 69.3 %shard_map.136 = bf16[16,2048]{1,0:T(8,128)(2,1)} custom-call(bf16[256,2048]{1,0:T(8,128)(2,1)} %tokens.1, s32[256,1]{1,0:T(8,128)} %copy.23.domain_ids, bf16[22,2048]{1,0:T(8,128)(2,1)} %domain_bias.1, bf16[2048,684]{1,0:T(8,128)(2,1)} %copy.24.dense_gate, bf16[2048,684]{1,0:T(8,128)(2,1)} %copy.25.dense_up, bf16[684,2048]{1,0:T(8,128)(2,1)} %dense_down.1, ...), custom_call_target="tpu_custom_call" | custom-call | flops 7134511104 | bytes 19218432 | tf_op jit(solution)/shard_map/pallas_call | solution.py:425
  93.3 1.5 %copy.33 = bf16[16,2048]{1,0:T(8,128)(2,1)} copy(bf16[16,2048]{1,0:T(8,128)(2,1)} %shard_map.136) | data formatting | bytes 131072
Async XLA Ops:
  0.0 9.0 %copy-start.1 = (bf16[2048,684]{0,1:T(8,128)(2,1)S(1)}, bf16[2048,684]{0,1:T(8,128)(2,1)}, u32[]{:S(2)}) copy-start(bf16[2048,684]{0,1:T(8,128)(2,1)} %param.17) | copy-start | bytes 8404996
  11.8 4.8 %copy-start = (bf16[1,2048,704]{1,2,0:T(8,128)(2,1)S(1)}, bf16[1,2048,704]{1,2,0:T(8,128)(2,1)}, u32[]{:S(2)}) copy-start(bf16[1,2048,704]{1,2,0:T(8,128)(2,1)} %param.23) | copy-start | bytes 8650756
